TPU v7x, 32 devices: a whole 2x2x4 slice. The times are simulated.
32 devices in a mesh: dp: 16 (over z, y, core), tensor: 2 (over x).
Axes of the slice: x: 2, y: 2, z: 4, core: 2. Of those that a mesh axis runs over, the one named last changes fastest.
Arguments:
- looked: bfloat16 [8192, 2048], P(('dp', 'tensor')), may hold values from -6 to 6
- column_owner: int32 [8192], replicated, may hold values from 0 to 8191, each once
- v_proj: bfloat16 [384, 8192], P(None, 'tensor'), may hold values from -0.0625 to 0.0625
- u_proj: bfloat16 [384, 8192], P(None, 'tensor'), may hold values from -0.3125 to 0.3125
- bias: float32 [8192], P('tensor'), may hold values from -3 to 3
- upstream: bfloat16 [8192, 2048], P('tensor', 'dp'), may hold values from -6 to 6
Outputs:
- d_looked: bfloat16 [8192, 2048], P(('dp', 'tensor'))
- grad_u: float32 [384, 8192], P('dp', 'tensor')
- grad_v: float32 [384, 8192], P('dp', 'tensor')
- grad_bias: float32 [8192], P('tensor')
Inputs may be any that keep to these rules, and one draw needn't show every extreme that they name: A permutation of the 8192 feature columns: wire row r carries column column_owner[r].
All inputs are finite; a program needn't handle non-finite values.
Results may differ from a plain program's by a relative error of at most 0.0049.
Values may be sent and summed in bfloat16 or wider, within the bound.
A program may use at most 128 MiB of HBM per device.

v0:
```python
import math

import jax
import jax.numpy as jnp
from jax import lax
from jax.sharding import PartitionSpec as P


def contract_last(left, right):
    return lax.dot_general(
        left, right, (((1,), (1,)), ((), ())), preferred_element_type=jnp.float32
    )


def contract_first(left, right):
    return lax.dot_general(
        left, right, (((0,), (0,)), ((), ())), preferred_element_type=jnp.float32
    )


def rank_cotangent(u_proj, scaled16):
    dh_part = jnp.dot(u_proj, scaled16, preferred_element_type=jnp.float32)
    return lax.psum(dh_part, "tensor").astype(jnp.bfloat16)


def per_device(looked, column_owner, v_proj, u_proj, bias, upstream):
    dp_count = lax.axis_size("dp")
    pair_count = lax.axis_size("tensor")
    pair_index = lax.axis_index("tensor")
    block_rows = looked.shape[0]
    half_width = v_proj.shape[1]
    full_width = half_width * pair_count
    local_samples = upstream.shape[1]
    norm = 1.0 / math.sqrt(local_samples * dp_count)
    wire_ids = jnp.arange(full_width, dtype=jnp.int32)
    inverse = jnp.zeros((full_width,), jnp.int32).at[column_owner].set(wire_ids)
    mine_wire = lax.dynamic_slice_in_dim(inverse, pair_index * half_width, half_width)
    arrived = lax.all_to_all(looked, "dp", split_axis=1, concat_axis=0, tiled=True)
    paired = lax.all_gather(arrived, "tensor", axis=0, tiled=True)
    block_ids = mine_wire // block_rows
    within = mine_wire % block_rows
    gather_rows = (
        block_ids % pair_count * (dp_count * block_rows)
        + block_ids // pair_count * block_rows
        + within
    )
    x_zero = jnp.take(paired, gather_rows, axis=0)
    h_part = jnp.dot(v_proj, x_zero, preferred_element_type=jnp.float32)
    hrank = lax.psum(h_part, "tensor").astype(jnp.bfloat16)
    mix = contract_first(u_proj, hrank) + bias[:, None]
    cotan = upstream.astype(jnp.float32)
    scaled = cotan * x_zero.astype(jnp.float32)
    scaled16 = scaled.astype(jnp.bfloat16)
    grad_bias = lax.psum(jnp.sum(scaled, axis=1), "dp") * norm
    dhrank = rank_cotangent(u_proj, scaled16)
    first = contract_last(hrank, scaled16)
    second = contract_last(dhrank, x_zero)
    joined_grads = (
        lax.psum_scatter(
            jnp.concatenate([first, second], axis=1), "dp", scatter_dimension=0, tiled=True
        )
        * norm
    )
    grad_u = joined_grads[:, :half_width]
    grad_v = joined_grads[:, half_width:]
    dx_zero = (cotan * (mix + 1.0) + contract_first(v_proj, dhrank)).astype(jnp.bfloat16)
    dx_full = lax.all_gather(dx_zero, "tensor", axis=0, tiled=True)
    send_wire = (
        (jnp.arange(dp_count, dtype=jnp.int32)[:, None] * pair_count + pair_index) * block_rows
        + jnp.arange(block_rows, dtype=jnp.int32)[None, :]
    ).reshape(-1)
    send_cols = jnp.take(column_owner, send_wire, axis=0)
    outgoing = jnp.take(dx_full, send_cols, axis=0)
    d_looked = lax.all_to_all(outgoing, "dp", split_axis=0, concat_axis=1, tiled=True)
    return (d_looked, grad_u, grad_v, grad_bias)


def solution(mesh):
    in_specs = (
        P(("dp", "tensor"), None),
        P(),
        P(None, "tensor"),
        P(None, "tensor"),
        P("tensor"),
        P("tensor", "dp"),
    )
    out_specs = (P(("dp", "tensor"), None), P("dp", "tensor"), P("dp", "tensor"), P("tensor"))
    return jax.shard_map(
        per_device, mesh=mesh, in_specs=in_specs, out_specs=out_specs, check_vma=False
    )
```

profile of v0, /device:TPU:0, one launch (start us, length us, event | category | flops | bytes accessed | tf_op | source)
XLA Modules:
  0.0 326.4 jit_solution(15770889080452752020)
XLA Ops:
  7.2 0.0 copy-start
  7.2 0.0 all-gather.3.cloned.1.call-start
  7.2 1.6 copy_bitcast_fusion.1
  8.9 32.1 %all_to_all.38 = bf16[256,16,128]{2,0,1:T(8,128)(2,1)} all-to-all(bf16[256,16,128]{2,0,1:T(8,128)(2,1)S(1)} %copy_bitcast_fusion.1), channel_id=1, replica_groups=mesh['dp'=16,'tensor'=2] {'dp'}, dimensions={1} | all-to-all | bytes 2097152 | tf_op jit(solution)/shard_map/all_to_all | solution.py:38
  41.0 0.0 copy-start.1
  41.0 0.0 all-gather.3.cloned.1.call-update
  41.0 0.0 all-gather.5.cloned.1.call-start
  41.1 2.3 copy.15
  43.4 0.0 copy-done.1
  43.4 30.5 %scatter_custom_fusion = s32[8192]{0:T(1024)S(1)} fusion(s32[8192]{0:T(1024)S(1)} %compare_select_fusion.1, s32[8192]{0:T(1024)S(1)} %iota.12, s32[]{:T(128)} %constant.77.clone.1), kind=kCustom, calls=%fused_computation.56 | custom fusion | bytes 32772 | tf_op jit(solution)/shard_map/scatter | solution.py:36
  73.9 0.1 compare_and_fusion.1
  73.9 0.7 all-gather.3.cloned.1.call-done
  74.6 16.1 %gather_fusion.1 = bf16[4096,128]{1,0:T(8,128)(2,1)} fusion(bf16[8192,128]{1,0:T(8,128)(2,1)} %all-gather.3.cloned.1.call-done, s32[4096]{0:T(1024)S(1)} %broadcast_clamp_fusion.1), kind=kCustom, calls=%fused_computation.clone | custom fusion | bytes 2113536 | tf_op jit(solution)/shard_map/jit(_take)/gather | solution.py:47
  90.7 2.3 copy.17
  93.0 0.0 copy-done
  93.0 0.0 copy-start.3
  93.0 0.0 copy-start.5
  93.0 3.4 %convolution_bitcast_fusion.1 = f32[384,128]{0,1:T(8,128)} fusion(bf16[384,4096]{1,0:T(8,128)(2,1)S(1)} %copy-done, bf16[4096,128]{0,1:T(8,128)(2,1)} %copy.15, bf16[4096,128]{0,1:T(8,128)(2,1)} %copy.17, pred[4096]{0:T(1024)(128)(4,1)S(1)} %get-tuple-element.7), kind=kOutput, calls=%fused_computation.15 | convolution fusion | flops 405274624 | bytes 5443584 | tf_op jit(solution)/shard_map/dot_general | solution.py:22
  96.4 0.0 copy-done.3
  96.4 0.0 copy-done.5
  96.4 0.0 copy-start.7
  96.4 1.8 convolution_bitcast_fusion.2
  98.2 16.2 %all-reduce.2 = (bf16[384,128]{0,1:T(8,128)(2,1)S(1)}, bf16[384,128]{0,1:T(8,128)(2,1)S(1)}) all-reduce(f32[384,128]{0,1:T(8,128)} %convolution_bitcast_fusion.2, f32[384,128]{0,1:T(8,128)} %convolution_bitcast_fusion.1), channel_id=1, replica_groups=mesh['dp'=16,'tensor'=2] {'tensor'}, use_global_device_ids=true, to_apply=%region_1.3 | all-reduce | flops 98304 | bytes 589824 | tf_op jit(solution)/shard_map/psum | solution.py:49
  114.4 0.0 copy-done.7
  114.4 0.0 copy-start.6
  114.4 2.1 fusion.3
  116.5 0.1 copy-done.6
  116.6 1.8 fusion.4
  118.4 0.0 all-gather.5.cloned.1.call-update
  118.4 0.0 reduce-scatter.2.cloned.1.call-start
  118.4 0.0 copy-start.2
  118.4 0.0 copy-start.4
  118.5 5.0 %fusion.7 = f32[384,4096]{1,0:T(8,128)} fusion(bf16[4096,128]{0,1:T(8,128)(2,1)} %copy.17, pred[4096]{0:T(1024)(128)(4,1)S(1)} %get-tuple-element.7, bf16[384,128]{0,1:T(8,128)(2,1)S(1)} %get-tuple-element.6), kind=kOutput, calls=%fused_computation.21 | convolution fusion | flops 403177472 | bytes 7442432 | tf_op jit(solution)/shard_map/dot_general | solution.py:10
  123.4 0.0 copy-done.2
  123.4 0.0 copy-done.4
  123.4 3.6 %fusion.10 = f32[384,4096]{1,0:T(8,128)} fusion(bf16[4096,128]{0,1:T(8,128)(2,1)S(1)} %copy-done.2, bf16[4096,128]{0,1:T(8,128)(2,1)S(1)} %copy-done.4, pred[4096]{0:T(1024)(128)(4,1)S(1)} %get-tuple-element.7, bf16[384,128]{0,1:T(8,128)(2,1)S(1)} %get-tuple-element.5), kind=kOutput, calls=%fused_computation.25 | convolution fusion | flops 405274624 | bytes 8491008 | tf_op jit(solution)/shard_map/dot_general | solution.py:10
  127.0 10.5 %pad_maximum_fusion = f32[384,8192]{1,0:T(8,128)} fusion(f32[384,4096]{1,0:T(8,128)} %fusion.7, f32[384,4096]{1,0:T(8,128)} %fusion.10), kind=kLoop, calls=%fused_computation.4 | loop fusion | flops 3145728 | bytes 25165824 | tf_op jit(solution)/shard_map/concatenate | solution.py:60
  137.6 0.0 reduce-scatter.2.cloned.1.call-update
  137.6 0.1 fusion.22
  137.8 23.0 %gather_fusion = s32[4096]{0:T(1024)S(1)} fusion(s32[8192]{0:T(1024)S(1)} %copy-done.1, s32[4096]{0:T(1024)S(1)} %broadcast_clamp_fusion.2), kind=kCustom, calls=%fused_computation.2 | custom fusion | bytes 49152 | tf_op jit(solution)/shard_map/jit(_take)/gather | solution.py:72
  160.9 0.0 all-gather.5.cloned.1.call-done
  160.9 4.2 %copy.18 = bf16[8192,128]{1,0:T(8,128)(2,1)} copy(bf16[8192,128]{0,1:T(8,128)(2,1)} %all-gather.5.cloned.1.call-done) | data formatting | bytes 4194304 | tf_op jit(solution)/shard_map/all_gather | solution.py:67
  165.1 16.4 %gather_fusion.2 = bf16[4096,128]{1,0:T(8,128)(2,1)} fusion(bf16[8192,128]{1,0:T(8,128)(2,1)} %copy.18, s32[4096]{0:T(1024)S(1)} %broadcast_clamp_fusion), kind=kCustom, calls=%fused_computation.1.clone | custom fusion | bytes 2113536 | tf_op jit(solution)/shard_map/jit(_take)/gather | solution.py:73
  181.5 4.2 %broadcast_select_fusion = bf16[4096,128]{1,0:T(8,128)(2,1)} fusion(bf16[4096,128]{1,0:T(8,128)(2,1)} %gather_fusion.2, pred[4096]{0:T(1024)(128)(4,1)S(1)} %compare_and_fusion), kind=kLoop, calls=%fused_computation.19 | loop fusion | flops 524288 | bytes 2101248 | tf_op jit(solution)/shard_map/jit(_take)/select_n | solution.py:73
  185.7 4.5 %all-to-all-start.1 = ((bf16[16,256,128]{2,1,0:T(8,128)(2,1)}), bf16[16,256,128]{2,1,0:T(8,128)(2,1)}, u32[]{:S(2)}, u32[]{:S(2)}) async-start(bf16[16,256,128]{2,1,0:T(8,128)(2,1)} %bitcast.48), calls=%async_computation.1 | async-start | bytes 2097152 | tf_op jit(solution)/shard_map/all_to_all | solution.py:74
  190.3 1.9 fusion.5
  192.2 91.3 %psum.23 = f32[4096]{0:T(1024)S(1)} all-reduce(f32[4096]{0:T(1024)S(1)} %fusion.5), channel_id=1, replica_groups=mesh['dp'=16,'tensor'=2] {'dp'}, use_global_device_ids=true, to_apply=%region_5.7 | all-reduce | flops 4096 | bytes 32768 | tf_op jit(solution)/shard_map/psum | solution.py:54
  283.5 0.6 broadcast_multiply_fusion.1
  284.1 0.0 all-to-all-done.1
  284.2 2.4 copy_bitcast_fusion
  286.5 31.3 %reduce-scatter.2.cloned.1.call-done = f32[24,8192]{1,0:T(8,128)} async-done(((f32[384,8192]{1,0:T(8,128)}), f32[24,8192]{1,0:T(8,128)}) %reduce-scatter.2.cloned.1.call-update) | async-done | bytes 786448 | tf_op jit(solution)/shard_map/reduce_scatter | solution.py:59
  317.8 1.2 broadcast_multiply_fusion
  319.0 0.9 fusion.35
  (10 shorter events, 0.1 us)
Async XLA Ops:
  7.2 85.8 %copy-start = (bf16[384,4096]{1,0:T(8,128)(2,1)S(1)}, bf16[384,4096]{1,0:T(8,128)(2,1)}, u32[]{:S(2)}) copy-start(bf16[384,4096]{1,0:T(8,128)(2,1)} %param.11) | copy-start | bytes 9437188
  7.2 67.4 %all-gather.3.cloned.1.call-start = ((), (), s32[]{:S(2)}) async-start(), calls=%async_computation.3 | async-start | bytes 3145728 | tf_op jit(solution)/shard_map/all_gather | solution.py:39
  41.0 2.4 copy-start.1
  41.0 119.8 %all-gather.5.cloned.1.call-start = ((), (), s32[]{:S(2)}) async-start(), calls=%async_computation.4 | async-start | bytes 3145728 | tf_op jit(solution)/shard_map/all_gather | solution.py:67
  93.0 3.5 %copy-start.3 = (bf16[4096,128]{0,1:T(8,128)(2,1)S(1)}, bf16[4096,128]{0,1:T(8,128)(2,1)}, u32[]{:S(2)}) copy-start(bf16[4096,128]{0,1:T(8,128)(2,1)} %copy.17) | copy-start | bytes 3145732
  93.0 3.5 %copy-start.5 = (bf16[384,4096]{1,0:T(8,128)(2,1)S(1)}, bf16[384,4096]{1,0:T(8,128)(2,1)}, u32[]{:S(2)}) copy-start(bf16[384,4096]{1,0:T(8,128)(2,1)} %param.10) | copy-start | bytes 9437188
  96.4 18.0 %copy-start.7 = (f32[4096]{0:T(1024)S(1)}, f32[4096]{0:T(1024)}, u32[]{:S(2)}) copy-start(f32[4096]{0:T(1024)} %param.12) | copy-start | bytes 49156
  114.4 2.2 copy-start.6
  118.4 199.4 %reduce-scatter.2.cloned.1.call-start = ((), (), s32[]{:S(2)}) async-start(), calls=%async_computation.5 | async-start | bytes 13369344 | tf_op jit(solution)/shard_map/reduce_scatter | solution.py:59
  118.4 5.0 %copy-start.2 = (bf16[4096,128]{0,1:T(8,128)(2,1)S(1)}, bf16[4096,128]{0,1:T(8,128)(2,1)}, u32[]{:S(2)}) copy-start(bf16[4096,128]{0,1:T(8,128)(2,1)} %copy.15) | copy-start | bytes 3145732
  118.4 5.0 %copy-start.4 = (bf16[4096,128]{0,1:T(8,128)(2,1)S(1)}, bf16[4096,128]{0,1:T(8,128)(2,1)}, u32[]{:S(2)}) copy-start(bf16[4096,128]{0,1:T(8,128)(2,1)} %copy.17) | copy-start | bytes 3145732
  185.7 98.4 %all-to-all-start.1 = ((bf16[16,256,128]{2,1,0:T(8,128)(2,1)}), bf16[16,256,128]{2,1,0:T(8,128)(2,1)}, u32[]{:S(2)}, u32[]{:S(2)}) async-start(bf16[16,256,128]{2,1,0:T(8,128)(2,1)} %bitcast.48), calls=%async_computation.1 | async-start | bytes 2097152 | tf_op jit(solution)/shard_map/all_to_all | solution.py:74
Sparse Core Ops, SparseCore 0:
  41.2 33.4 all-gather.2
  118.5 31.8 all-gather.4
  154.4 163.2 reduce-scatter.1
where the time goes:
time: 327 us; the launch traced here: 326 us
  blocking collectives  140 us (43%)
  local copies, waits for them, and re-layouts  99.8 us (31%)
  waiting for transfers between devices  32 us (10%)
  other arithmetic  18.7 us (6%)
  matrix products  17.6 us (5%)
  between operations  13.9 us (4%)
  starting transfers between devices  4.66 us (1%)
    psum x1, blocking collectives, per_device(): grad_bias = lax.psum(jnp.sum(scaled, axis=1), 'dp') * norm  91.3 us
    all_to_all x1, blocking collectives, per_device(): lax.all_to_all(looked, 'dp', split_axis=1, concat_axis=0, tiled=True)  32.1 us
    reduce_scatter x1, waiting for transfers between devices, per_device(): lax.psum_scatter(jnp.concatenate([first, second], axis=1), 'dp', scatter_...  31.3 us
    scatter x1, local copies, waits for them, and re-layouts, per_device(): inverse = jnp.zeros((full_width,), jnp.int32).at[column_owner].set(wire_ids)  30.5 us
    gather x1, local copies, waits for them, and re-layouts, per_device(): send_cols = jnp.take(column_owner, send_wire, axis=0)  23 us
    gather x2, local copies, waits for them, and re-layouts, per_device(): x_zero = jnp.take(paired, gather_rows, axis=0)  18.4 us
    gather x1, local copies, waits for them, and re-layouts, per_device(): outgoing = jnp.take(dx_full, send_cols, axis=0)  16.4 us
    psum x1, blocking collectives, per_device(): hrank = lax.psum(h_part, 'tensor').astype(jnp.bfloat16)  16.2 us
  transfers between devices with their start and end apart: 4, of which 2 were waited for; matrix products, arithmetic and copies ran while one was open for 32% of the time, Pallas kernels for 0%

commit v1 on v0

v1 whole, which is shorter than its diff:
```python
import functools
import math

import jax
import jax.numpy as jnp
from jax import lax
from jax.experimental import pallas as pl
from jax.experimental.pallas import tpu as pltpu
from jax.sharding import PartitionSpec as P

BOTH = ("dp", "tensor")


def gather_kernel(ids_ref, src_ref, out_ref, wide, picked):
    rows = out_ref.shape[0]
    wide[...] = src_ref[...].astype(jnp.float32)
    step = 32

    def body(i, carry):
        base = pl.multiple_of(i * step, step)
        for k in range(step):
            picked[pl.ds(base + k, 1), :] = wide[pl.ds(ids_ref[base + k], 1), :]
        return carry

    lax.fori_loop(0, rows // step, body, 0)
    out_ref[...] = picked[...].astype(jnp.bfloat16)


def gather_rows(ids, src, rows):
    lanes = src.shape[1]
    return pl.pallas_call(
        gather_kernel,
        out_shape=jax.ShapeDtypeStruct((rows, lanes), jnp.bfloat16),
        in_specs=[
            pl.BlockSpec(memory_space=pltpu.SMEM),
            pl.BlockSpec(memory_space=pltpu.VMEM),
        ],
        out_specs=pl.BlockSpec(memory_space=pltpu.VMEM),
        scratch_shapes=[
            pltpu.VMEM(src.shape, jnp.float32),
            pltpu.VMEM((rows, lanes), jnp.float32),
        ],
        compiler_params=pltpu.CompilerParams(vmem_limit_bytes=48 * 2**20),
        cost_estimate=pl.CostEstimate(flops=0, bytes_accessed=20 * 2**20, transcendentals=0),
    )(ids, src)


def scatter_kernel(ids_ref, src_ref, out_ref):
    rows = src_ref.shape[0]
    step = 32

    def body(i, carry):
        base = pl.multiple_of(i * step, step)
        for k in range(step):
            out_ref[pl.ds(ids_ref[base + k], 1), :] = src_ref[pl.ds(base + k, 1), :]
        return carry

    lax.fori_loop(0, rows // step, body, 0)


def scatter_rows(ids, src, rows):
    return pl.pallas_call(
        scatter_kernel,
        out_shape=jax.ShapeDtypeStruct((rows, src.shape[1]), jnp.float32),
        in_specs=[
            pl.BlockSpec(memory_space=pltpu.SMEM),
            pl.BlockSpec(memory_space=pltpu.VMEM),
        ],
        out_specs=pl.BlockSpec(memory_space=pltpu.VMEM),
        compiler_params=pltpu.CompilerParams(vmem_limit_bytes=48 * 2**20),
        cost_estimate=pl.CostEstimate(flops=0, bytes_accessed=20 * 2**20, transcendentals=0),
    )(ids, src)


def dot(left, right, dims):
    return lax.dot_general(left, right, (dims, ((), ())), preferred_element_type=jnp.float32)


def to_owner(parts, pair_count, pair_index):
    total = lax.dynamic_index_in_dim(parts, pair_index, 0, keepdims=False)
    for shift in range(1, pair_count):
        other = lax.rem(pair_index + shift, pair_count)
        sent = lax.dynamic_index_in_dim(parts, other, 0, keepdims=False)
        total = total + lax.ppermute(
            sent, "tensor", [(i, (i + shift) % pair_count) for i in range(pair_count)]
        )
    return total


def all_sum(part):
    mine = lax.psum_scatter(part, BOTH, scatter_dimension=0, tiled=True)
    return lax.all_gather(mine.astype(jnp.bfloat16), BOTH, axis=0, tiled=True)


def per_device(looked, column_owner, v_proj, u_proj, bias, upstream):
    dp_count = lax.axis_size("dp")
    pair_count = lax.axis_size("tensor")
    dp_index = lax.axis_index("dp")
    pair_index = lax.axis_index("tensor")
    own, samples = looked.shape
    rank, half = v_proj.shape
    norm = 1.0 / math.sqrt(samples)
    blocks = column_owner.reshape(dp_count, pair_count, own)

    group = lax.dynamic_index_in_dim(blocks, dp_index, 0, keepdims=False) - pair_index * half
    hit = jnp.arange(half, dtype=jnp.int32)[:, None] == group.reshape(1, -1)
    both = jnp.concatenate([v_proj, u_proj], axis=0)
    picked = jnp.dot(both, hit.astype(jnp.bfloat16), preferred_element_type=jnp.float32)
    picked = picked.astype(jnp.bfloat16).reshape(2 * rank, pair_count, own).transpose(1, 0, 2)
    params = to_owner(picked, pair_count, pair_index)
    v_own, u_own = params[:rank], params[rank:]
    bias_parts = jnp.sum(jnp.where(hit, bias[:, None], 0.0), axis=0).reshape(pair_count, own)
    bias_own = to_owner(bias_parts, pair_count, pair_index)

    paired = lax.all_gather(upstream, "tensor", axis=0, tiled=True)
    wanted = lax.dynamic_index_in_dim(blocks, pair_index, 1, keepdims=False).reshape(-1)
    wired = gather_rows(wanted, paired, half)
    cotan16 = lax.all_to_all(wired, "dp", split_axis=0, concat_axis=1, tiled=True)

    hrank = all_sum(dot(looked, v_own, ((0,), (1,))))
    cotan = cotan16.astype(jnp.float32)
    scaled = cotan * looked.astype(jnp.float32)
    scaled16 = scaled.astype(jnp.bfloat16)
    sums = jnp.sum(scaled, axis=1)
    dhrank = all_sum(dot(scaled16, u_own, ((0,), (1,))))

    mix = dot(u_own, hrank, ((0,), (1,))) + bias_own[:, None]
    d_looked = (cotan * (mix + 1.0) + dot(v_own, dhrank, ((0,), (1,)))).astype(jnp.bfloat16)

    own_u = dot(hrank, scaled16, ((0,), (1,))).reshape(dp_count, -1, own)
    own_v = dot(dhrank, looked, ((0,), (1,))).reshape(dp_count, -1, own)
    each = rank // dp_count
    fill = -(-(2 * each + 1) // 8) * 8 - 2 * each
    own_b = jnp.broadcast_to(sums[None, None, :], (dp_count, fill, own))
    sent = jnp.concatenate([own_u, own_v, own_b], axis=1) * norm
    came = lax.all_to_all(sent, "dp", split_axis=0, concat_axis=0, tiled=True)
    full = lax.all_gather(came, "tensor", axis=1, tiled=False)
    lines = full.transpose(0, 1, 3, 2).reshape(half * pair_count, -1)
    lines = jnp.pad(lines, ((0, 0), (0, 128 - lines.shape[1])))
    place = column_owner - pair_index * half
    place = jnp.where((place >= 0) & (place < half), place, half)
    spread = scatter_rows(place, lines, half + 8)[:half].T
    return (d_looked, spread[:each], spread[each : 2 * each], spread[2 * each])


def solution(mesh):
    in_specs = (
        P(BOTH, None),
        P(),
        P(None, "tensor"),
        P(None, "tensor"),
        P("tensor"),
        P("tensor", "dp"),
    )
    out_specs = (P(BOTH, None), P("dp", "tensor"), P("dp", "tensor"), P("tensor"))
    return jax.shard_map(
        per_device, mesh=mesh, in_specs=in_specs, out_specs=out_specs, check_vma=False
    )
```

time: 327 us -> 457 us (1.40)
  waiting for transfers between devices: 32 us -> 319 us
  blocking collectives: 140 us -> 57.8 us
  local copies, waits for them, and re-layouts: 99.8 us -> 21.9 us
  Pallas kernels: 0 us -> 14.7 us
  other arithmetic: 18.7 us -> 4.67 us
    all_gather x2 -> x4, waiting for transfers between devices: 0.69 us -> 143 us  [the longest x2 111 us: all_sum(): return lax.all_gather(mine.astype(jnp.bfloat16), BOTH, axis=0, tiled=True)]
    reduce_scatter x1 -> x2, waiting for transfers between devices: 31.3 us -> 157 us  [all_sum(): mine = lax.psum_scatter(part, BOTH, scatter_dimension=0, tiled=True)]
    psum x2 -> x0, blocking collectives: 108 us -> none  [the longest x1 91.3 us: per_device(): grad_bias = lax.psum(jnp.sum(scaled, axis=1), 'dp') * norm]
    gather x4 -> x0, local copies, waits for them, and re-layouts: 57.8 us -> none  [the longest x1 23 us: per_device(): send_cols = jnp.take(column_owner, send_wire, axis=0)]
    scatter x1 -> x0, local copies, waits for them, and re-layouts: 30.5 us -> none  [per_device(): inverse = jnp.zeros((full_width,), jnp.int32).at[column_owner].set(wire_ids)]
    all_to_all x1 -> x2, blocking collectives: 32.1 us -> 57.8 us  [the longest x1 30.8 us: per_device(): lax.all_to_all(wired, 'dp', split_axis=0, concat_axis=1, tiled=True)]
    ppermute x0 -> x2, waiting for transfers between devices: none -> 18.6 us  [to_owner(): lax.ppermute(sent, 'tensor', [(i, (i + shift) % pair_count) for i in rang...]
    pallas_call x0 -> x2, Pallas kernels: none -> 14.7 us  [the longest x1 9.74 us: scatter_rows(): pl.pallas_call(scatter_kernel, out_shape=jax.ShapeDtypeStruct((rows, src....]
  transfers between devices with their start and end apart: 4 -> 8, of which waited for: 2 -> 8; matrix products, arithmetic and copies ran while one was open for 32% -> 5% of each run, Pallas kernels for 0% -> 1%
where the time goes in v1:
time: 457 us; the launch traced here: 456 us
  waiting for transfers between devices  319 us (70%)
  blocking collectives  57.8 us (13%)
  local copies, waits for them, and re-layouts  21.9 us (5%)
  matrix products  18.9 us (4%)
  between operations  15.9 us (3%)
  Pallas kernels  14.7 us (3%)
  other arithmetic  4.67 us (1%)
    reduce_scatter x2, waiting for transfers between devices, all_sum(): mine = lax.psum_scatter(part, BOTH, scatter_dimension=0, tiled=True)  157 us
    all_gather x2, waiting for transfers between devices, all_sum(): return lax.all_gather(mine.astype(jnp.bfloat16), BOTH, axis=0, tiled=True)  111 us
    all_to_all x1, blocking collectives, per_device(): lax.all_to_all(wired, 'dp', split_axis=0, concat_axis=1, tiled=True)  30.8 us
    all_to_all x1, blocking collectives, per_device(): came = lax.all_to_all(sent, 'dp', split_axis=0, concat_axis=0, tiled=True)  27 us
    all_gather x1, waiting for transfers between devices, per_device(): full = lax.all_gather(came, 'tensor', axis=1, tiled=False)  20.3 us
    ppermute x2, waiting for transfers between devices, to_owner(): lax.ppermute(sent, 'tensor', [(i, (i + shift) % pair_count) for i in rang...  18.6 us
    dot_general x6, matrix products, dot(): lax.dot_general(left, right, (dims, ((), ())), preferred_element_type=jnp...  12.4 us
    all_gather x1, waiting for transfers between devices, per_device(): paired = lax.all_gather(upstream, 'tensor', axis=0, tiled=True)  11.1 us
  transfers between devices with their start and end apart: 8, of which 8 were waited for; matrix products, arithmetic and copies ran while one was open for 5% of the time, Pallas kernels for 1%

profile of v1, /device:TPU:0, one launch (start us, length us, event | category | flops | bytes accessed | tf_op | source)
XLA Modules:
  0.0 456.3 jit_solution(5029394830418690842)
XLA Ops:
  8.0 0.0 all-gather.6.cloned.1.call-start
  8.0 0.7 all-gather.6.cloned.1.call-update
  8.7 0.0 reduce-scatter.7.cloned.1.call-start
  8.8 0.8 reshape.50
  9.6 0.0 copy-start.4
  9.6 6.5 %fusion.9 = bf16[768,512]{0,1:T(8,128)(2,1)S(1)} fusion(s32[512]{0:T(512)S(1)} %bitcast.56, bf16[384,4096]{1,0:T(8,128)(2,1)} %param.9, bf16[384,4096]{1,0:T(8,128)(2,1)} %param.8), kind=kOutput, calls=%fused_computation.17 | convolution fusion | flops 3236298752 | bytes 7079936 | tf_op jit(solution)/shard_map/dot_general | solution.py:108
  16.1 0.0 copy-done.4
  16.2 3.0 collective-permute-start
  19.2 15.7 %collective-permute-done = bf16[768,256]{0,1:T(8,128)(2,1)S(1)} collective-permute-done((bf16[768,256]{0,1:T(8,128)(2,1)S(1)}, bf16[768,256]{0,1:T(8,128)(2,1)S(1)}, u32[]{:S(2)}, u32[]{:S(2)}) %collective-permute-start) | collective-permute-done | bytes 393248 | tf_op jit(solution)/shard_map/ppermute | solution.py:84
  35.0 1.8 convolution_bitcast_fusion
  36.8 2.4 copy.32
  39.2 0.0 copy-start.5
  39.2 0.0 reduce-scatter.7.cloned.1.call-update
  39.2 0.0 reduce-scatter.5.cloned.1.call-start
  39.2 0.7 copy-done.5
  39.9 11.1 %all-gather.6.cloned.1.call-done.src_ref = bf16[8192,128]{1,0:T(8,128)(2,1)} async-done(((bf16[4096,128]{1,0:T(8,128)(2,1)}), bf16[8192,128]{1,0:T(8,128)(2,1)}) %all-gather.6.cloned.1.call-update) | async-done | bytes 2097168 | tf_op jit(solution)/shard_map/all_gather | solution.py:115
  51.0 0.0 copy-start
  51.0 1.6 copy-done
  52.6 0.0 copy-start.1
  52.7 4.9 %shard_map.93 = bf16[4096,128]{1,0:T(8,128)(2,1)S(1)} custom-call(s32[4096]{0:T(1024)S(1)} %bitcast.48, bf16[8192,128]{1,0:T(8,128)(2,1)S(1)} %copy-done), custom_call_target="tpu_custom_call" | custom-call | bytes 20971520 | tf_op jit(solution)/shard_map/pallas_call | solution.py:31
  57.6 30.8 %all_to_all.18 = bf16[16,256,128]{2,1,0:T(8,128)(2,1)S(1)} all-to-all(bf16[16,256,128]{2,1,0:T(8,128)(2,1)S(1)} %bitcast.47), channel_id=1, replica_groups=mesh['dp'=16,'tensor'=2] {'dp'}, dimensions={0} | all-to-all | bytes 2097152 | tf_op jit(solution)/shard_map/all_to_all | solution.py:118
  88.4 0.0 copy-done.1
  88.5 2.4 fusion.17
  90.8 0.0 reduce-scatter.5.cloned.1.call-update
  90.9 0.0 all-gather.8.cloned.1.call-start
  90.9 52.3 %reduce-scatter.7.cloned.1.call-done = f32[64,384]{1,0:T(8,128)} async-done(((f32[2048,384]{1,0:T(8,128)}), f32[64,384]{1,0:T(8,128)}) %reduce-scatter.7.cloned.1.call-update) | async-done | bytes 98320 | tf_op jit(solution)/shard_map/reduce_scatter | solution.py:91
  143.2 1.5 convert_element_type.34
  144.7 0.0 all-gather.8.cloned.1.call-update
  144.7 0.0 all-gather.10.cloned.1.call-start
  144.8 104.2 %reduce-scatter.5.cloned.1.call-done = f32[64,384]{1,0:T(8,128)} async-done(((f32[2048,384]{1,0:T(8,128)}), f32[64,384]{1,0:T(8,128)}) %reduce-scatter.5.cloned.1.call-update) | async-done | bytes 98320 | tf_op jit(solution)/shard_map/reduce_scatter | solution.py:91
  249.0 1.5 convert_element_type.37
  250.6 0.0 all-gather.10.cloned.1.call-update
  250.6 0.0 all-gather.12.cloned.1.call-start
  250.6 0.4 fusion.12
  251.0 55.6 %all-gather.8.cloned.1.call-done = bf16[2048,384]{1,0:T(8,128)(2,1)} async-done(((bf16[64,384]{1,0:T(8,128)(2,1)}), bf16[2048,384]{1,0:T(8,128)(2,1)}) %all-gather.8.cloned.1.call-update) | async-done | bytes 1572880 | tf_op jit(solution)/shard_map/all_gather | solution.py:92
  306.5 2.0 fusion.21
  308.6 55.6 %all-gather.10.cloned.1.call-done = bf16[2048,384]{1,0:T(8,128)(2,1)} async-done(((bf16[64,384]{1,0:T(8,128)(2,1)}), bf16[2048,384]{1,0:T(8,128)(2,1)}) %all-gather.10.cloned.1.call-update) | async-done | bytes 1572880 | tf_op jit(solution)/shard_map/all_gather | solution.py:92
  364.2 2.0 fusion.25
  366.2 0.0 copy-start.6
  366.2 0.0 copy-start.3
  366.3 0.1 maximum_multiply_fusion
  366.3 27.0 %all_to_all.19 = f32[16,56,256]{2,1,0:T(8,128)} all-to-all(f32[16,56,256]{2,1,0:T(8,128)S(1)} %maximum_multiply_fusion), channel_id=1, replica_groups=mesh['dp'=16,'tensor'=2] {'dp'}, dimensions={0} | all-to-all | bytes 1835008 | tf_op jit(solution)/shard_map/all_to_all | solution.py:136
  393.3 0.0 all-gather.12.cloned.1.call-update
  393.3 0.0 copy-done.6
  393.3 0.0 copy-start.2
  393.4 1.1 select_reduce_fusion
  394.5 0.7 collective-permute-start.1
  395.2 0.0 copy-done.3
  395.2 2.9 collective-permute-done.1
  398.1 2.3 fusion.14
  400.4 0.0 copy-done.2
  400.4 1.8 fusion.8
  402.3 20.3 %all-gather.12.cloned.1.call-done = f32[16,112,256]{2,1,0:T(8,128)} async-done(((f32[16,56,256]{2,1,0:T(8,128)}), f32[16,112,256]{2,1,0:T(8,128)}) %all-gather.12.cloned.1.call-update) | async-done | bytes 1835024 | tf_op jit(solution)/shard_map/all_gather | solution.py:137
  422.6 3.7 copy.29
  426.3 4.4 pad.4.src_ref
  430.8 9.7 %shard_map.94 = f32[4104,128]{1,0:T(8,128)S(1)} custom-call(s32[8192]{0:T(1024)S(1)} %and_select_fusion.ids_ref, f32[8192,128]{1,0:T(8,128)} %pad.4.src_ref), custom_call_target="tpu_custom_call" | custom-call | bytes 20971520 | tf_op jit(solution)/shard_map/pallas_call | solution.py:62
  440.5 0.1 slice_bitcast_fusion
  440.7 1.8 slice_reduce_fusion
  442.4 2.0 fusion.24
  444.4 2.9 copy.31
  447.3 1.3 copy.30
  (10 shorter events, 0.2 us)
Async XLA Ops:
  8.0 43.0 %all-gather.6.cloned.1.call-start = ((), (), s32[]{:S(2)}) async-start(), calls=%async_computation.4 | async-start | bytes 3145728 | tf_op jit(solution)/shard_map/all_gather | solution.py:115
  8.7 134.5 %reduce-scatter.7.cloned.1.call-start = ((), (), s32[]{:S(2)}) async-start(), calls=%async_computation.9 | async-start | bytes 3244032 | tf_op jit(solution)/shard_map/reduce_scatter | solution.py:91
  9.6 6.6 %copy-start.4 = (s32[16,2,256]{2,1,0:T(2,128)}, s32[16,2,256]{2,1,0:T(2,128)S(1)}, u32[]{:S(2)}) copy-start(s32[16,2,256]{2,1,0:T(2,128)S(1)} %reshape.50) | copy-start | bytes 98308
  16.2 18.7 %collective-permute-start = (bf16[768,256]{0,1:T(8,128)(2,1)S(1)}, bf16[768,256]{0,1:T(8,128)(2,1)S(1)}, u32[]{:S(2)}, u32[]{:S(2)}) collective-permute-start(bf16[768,256]{0,1:T(8,128)(2,1)S(1)} %dynamic-slice_bitcast_fusion), channel_id=1, source_target_pairs={{0,1},{1,0},{2,3},{3,2},{4,5},{5,4},{6,7},{7,6},{8,9},{9,8},{10,11... | collective-permute-start | bytes 1179656 | tf_op jit(solution)/shard_map/ppermute | solution.py:84
  39.2 0.8 copy-start.5
  39.2 209.8 %reduce-scatter.5.cloned.1.call-start = ((), (), s32[]{:S(2)}) async-start(), calls=%async_computation.6 | async-start | bytes 3244032 | tf_op jit(solution)/shard_map/reduce_scatter | solution.py:91
  51.0 1.6 copy-start
  52.6 35.8 %copy-start.1 = (bf16[256,2048]{1,0:T(8,128)(2,1)S(1)}, bf16[256,2048]{1,0:T(8,128)(2,1)}, u32[]{:S(2)}) copy-start(bf16[256,2048]{1,0:T(8,128)(2,1)} %param.6) | copy-start | bytes 3145732
  90.9 215.7 %all-gather.8.cloned.1.call-start = ((), (), s32[]{:S(2)}) async-start(), calls=%async_computation.5 | async-start | bytes 1622016 | tf_op jit(solution)/shard_map/all_gather | solution.py:92
  144.7 219.4 %all-gather.10.cloned.1.call-start = ((), (), s32[]{:S(2)}) async-start(), calls=%async_computation.7 | async-start | bytes 1622016 | tf_op jit(solution)/shard_map/all_gather | solution.py:92
  250.6 172.0 %all-gather.12.cloned.1.call-start = ((), (), s32[]{:S(2)}) async-start(), calls=%async_computation.8 | async-start | bytes 2752512 | tf_op jit(solution)/shard_map/all_gather | solution.py:137
  366.2 27.1 %copy-start.6 = (f32[4096]{0:T(1024)S(1)}, f32[4096]{0:T(1024)}, u32[]{:S(2)}) copy-start(f32[4096]{0:T(1024)} %param.10) | copy-start | bytes 49156
  366.2 29.0 %copy-start.3 = (s32[8192]{0:T(1024)S(1)}, s32[8192]{0:T(1024)}, u32[]{:S(2)}) copy-start(s32[8192]{0:T(1024)} %param.7) | copy-start | bytes 98308
  393.3 7.1 %copy-start.2 = (bf16[2048,384]{1,0:T(8,128)(2,1)S(1)}, bf16[2048,384]{1,0:T(8,128)(2,1)}, u32[]{:S(2)}) copy-start(bf16[2048,384]{1,0:T(8,128)(2,1)} %all-gather.8.cloned.1.call-done) | copy-start | bytes 4718596
  394.5 3.6 collective-permute-start.1
Sparse Core Ops, SparseCore 0:
  10.4 40.5 all-gather.5
  393.5 29.0 all-gather.11
Sparse Core Ops, SparseCore 1:
  39.3 103.9 reduce-scatter.6
  148.5 100.5 reduce-scatter.4
  252.4 54.1 all-gather.7
  310.0 54.1 all-gather.9

commit v2 on v1

--- a/solution.py
+++ b/solution.py
@@ -87,9 +87,127 @@
     return total
 
 
-def all_sum(part):
-    mine = lax.psum_scatter(part, BOTH, scatter_dimension=0, tiled=True)
-    return lax.all_gather(mine.astype(jnp.bfloat16), BOTH, axis=0, tiled=True)
+def exchange_orders(dp_count, pair_count):
+    def strides(count):
+        return [1 << k for k in range(count.bit_length() - 1)]
+
+    inner, *outer = [("dp", p) for p in strides(dp_count)]
+    pair = [("tensor", p) for p in strides(pair_count)]
+    return ([inner] + pair + outer, [inner] + outer[:-1] + pair + outer[-1:])
+
+
+def sum_kernel(orders, part_ref, out_ref, *scratch):
+    steps = len(orders[0])
+    lanes = len(orders)
+    took = scratch[:steps]
+    given = scratch[steps : 2 * steps - 1]
+    held = scratch[2 * steps - 1 : 3 * steps - 1]
+    send_sem, recv_sem = scratch[3 * steps - 1 :]
+    rows = part_ref.shape[0] // lanes
+
+    def partner(axis, stride):
+        me = lax.axis_index(axis)
+        bit = lax.rem(me // stride, 2)
+        return bit, {axis: me + stride * (1 - 2 * bit)}
+
+    barrier = pltpu.get_barrier_semaphore()
+    for axis, stride in orders[0]:
+        pl.semaphore_signal(
+            barrier, inc=1, device_id=partner(axis, stride)[1], device_id_type=pl.DeviceIdType.MESH
+        )
+    pl.semaphore_wait(barrier, steps)
+
+    starts = [lane * rows for lane in range(lanes)]
+    for k in range(steps):
+        size = rows >> (k + 1)
+        copies = []
+        for lane in range(lanes):
+            bit, device = partner(*orders[lane][k])
+            away = pl.multiple_of((1 - bit) * size, size)
+            if k == 0:
+                source = part_ref.at[pl.ds(pl.multiple_of(lane * rows + away, size), size)]
+            else:
+                source = given[k - 1].at[lane]
+                source[...] = held[k - 1][lane, pl.ds(away, size), :].astype(jnp.bfloat16)
+            copy = pltpu.make_async_remote_copy(
+                src_ref=source,
+                dst_ref=took[k].at[lane],
+                send_sem=send_sem.at[lane, k],
+                recv_sem=recv_sem.at[lane, k],
+                device_id=device,
+                device_id_type=pl.DeviceIdType.MESH,
+            )
+            copy.start()
+            copies.append(copy)
+        for lane in range(lanes):
+            bit, _ = partner(*orders[lane][k])
+            kept = pl.multiple_of(bit * size, size)
+            copies[lane].wait()
+            if k == 0:
+                own = part_ref[pl.ds(pl.multiple_of(lane * rows + kept, size), size), :]
+            else:
+                own = held[k - 1][lane, pl.ds(kept, size), :]
+            held[k][lane] = own + took[k][lane].astype(jnp.float32)
+            starts[lane] = starts[lane] + kept
+
+    size = rows >> steps
+    for lane in range(lanes):
+        out_ref[pl.ds(pl.multiple_of(starts[lane], size), size), :] = held[-1][lane].astype(
+            jnp.bfloat16
+        )
+    for k in reversed(range(steps)):
+        size = rows >> (k + 1)
+        copies = []
+        for lane in range(lanes):
+            bit, device = partner(*orders[lane][k])
+            piece = out_ref.at[pl.ds(pl.multiple_of(starts[lane], size), size)]
+            copy = pltpu.make_async_remote_copy(
+                src_ref=piece,
+                dst_ref=piece,
+                send_sem=send_sem.at[lane, steps + k],
+                recv_sem=recv_sem.at[lane, steps + k],
+                device_id=device,
+                device_id_type=pl.DeviceIdType.MESH,
+            )
+            copy.start()
+            copies.append(copy)
+            starts[lane] = starts[lane] - bit * size
+        for copy in copies:
+            copy.wait()
+
+
+def all_sum(part, dp_count, pair_count):
+    orders = exchange_orders(dp_count, pair_count)
+    steps, lanes = len(orders[0]), len(orders)
+    samples, rank = part.shape
+    chunk = min(samples, max(2048, (16 * lanes) << steps))
+    rows = chunk // lanes
+
+    def shapes(kind, first, last):
+        return [pltpu.VMEM((lanes, rows >> (k + 1), rank), kind) for k in range(first, last)]
+
+    call = pl.pallas_call(
+        functools.partial(sum_kernel, orders),
+        out_shape=jax.ShapeDtypeStruct((chunk, rank), jnp.bfloat16),
+        in_specs=[pl.BlockSpec(memory_space=pltpu.VMEM)],
+        out_specs=pl.BlockSpec(memory_space=pltpu.VMEM),
+        scratch_shapes=[
+            *shapes(jnp.float32, 0, 1),
+            *shapes(jnp.bfloat16, 1, steps),
+            *shapes(jnp.bfloat16, 1, steps),
+            *shapes(jnp.float32, 0, steps),
+            pltpu.SemaphoreType.DMA((lanes, 2 * steps)),
+            pltpu.SemaphoreType.DMA((lanes, 2 * steps)),
+        ],
+        compiler_params=pltpu.CompilerParams(
+            collective_id=1, has_side_effects=True, vmem_limit_bytes=56 * 2**20
+        ),
+        cost_estimate=pl.CostEstimate(
+            flops=samples * rank, bytes_accessed=30 * 2**20, transcendentals=0
+        ),
+    )
+    pieces = [call(part[at : at + chunk]) for at in range(0, samples, chunk)]
+    return jnp.concatenate(pieces, axis=0) if len(pieces) > 1 else pieces[0]
 
 
 def per_device(looked, column_owner, v_proj, u_proj, bias, upstream):
@@ -117,12 +235,12 @@
     wired = gather_rows(wanted, paired, half)
     cotan16 = lax.all_to_all(wired, "dp", split_axis=0, concat_axis=1, tiled=True)
 
-    hrank = all_sum(dot(looked, v_own, ((0,), (1,))))
+    hrank = all_sum(dot(looked, v_own, ((0,), (1,))), dp_count, pair_count)
     cotan = cotan16.astype(jnp.float32)
     scaled = cotan * looked.astype(jnp.float32)
     scaled16 = scaled.astype(jnp.bfloat16)
     sums = jnp.sum(scaled, axis=1)
-    dhrank = all_sum(dot(scaled16, u_own, ((0,), (1,))))
+    dhrank = all_sum(dot(scaled16, u_own, ((0,), (1,))), dp_count, pair_count)
 
     mix = dot(u_own, hrank, ((0,), (1,))) + bias_own[:, None]
     d_looked = (cotan * (mix + 1.0) + dot(v_own, dhrank, ((0,), (1,)))).astype(jnp.bfloat16)

time: 457 us -> 263 us (0.58)
  waiting for transfers between devices: 319 us -> 71.5 us
  Pallas kernels: 14.7 us -> 104 us
  blocking collectives: 57.8 us -> 26.7 us
    reduce_scatter x2 -> x0, waiting for transfers between devices: 157 us -> none  [all_sum(): mine = lax.psum_scatter(part, BOTH, scatter_dimension=0, tiled=True)]
    all_gather x2 -> x0, waiting for transfers between devices: 111 us -> none  [all_sum(): return lax.all_gather(mine.astype(jnp.bfloat16), BOTH, axis=0, tiled=True)]
    pallas_call x0 -> x2, Pallas kernels: none -> 88.7 us  [all_sum(): pieces = [call(part[at:at + chunk]) for at in range(0, samples, chunk)]]
    all_to_all x1 -> x0, blocking collectives: 30.8 us -> none  [per_device(): lax.all_to_all(wired, 'dp', split_axis=0, concat_axis=1, tiled=True)]
    all_gather x1, waiting for transfers between devices: 11.1 us -> 36.7 us  [per_device(): paired = lax.all_gather(upstream, 'tensor', axis=0, tiled=True)]
    all_to_all x0 -> x1, starting transfers between devices: none -> 5.62 us  [per_device(): lax.all_to_all(wired, 'dp', split_axis=0, concat_axis=1, tiled=True)]
    ppermute x2, waiting for transfers between devices: 18.6 us -> 13.6 us  [to_owner(): lax.ppermute(sent, 'tensor', [(i, (i + shift) % pair_count) for i in rang...]
  transfers between devices with their start and end apart: 8 -> 5, of which waited for: 8 -> 4; matrix products, arithmetic and copies ran while one was open for 5% -> 6% of each run, Pallas kernels for 1% -> 17%
where the time goes in v2:
time: 263 us
  Pallas kernels  104 us (40%)
  waiting for transfers between devices  71.5 us (27%)
  blocking collectives  26.7 us (10%)
  local copies, waits for them, and re-layouts  18.8 us (7%)
  matrix products  18.2 us (7%)
  between operations  14.3 us (5%)
  starting transfers between devices  7.27 us (3%)
    pallas_call x2, Pallas kernels, all_sum(): pieces = [call(part[at:at + chunk]) for at in range(0, samples, chunk)]  88.7 us
    all_gather x1, waiting for transfers between devices, per_device(): paired = lax.all_gather(upstream, 'tensor', axis=0, tiled=True)  36.7 us
    all_to_all x1, blocking collectives, per_device(): came = lax.all_to_all(sent, 'dp', split_axis=0, concat_axis=0, tiled=True)  26.7 us
    all_gather x1, waiting for transfers between devices, per_device(): full = lax.all_gather(came, 'tensor', axis=1, tiled=False)  20.6 us
    ppermute x2, waiting for transfers between devices, to_owner(): lax.ppermute(sent, 'tensor', [(i, (i + shift) % pair_count) for i in rang...  13.6 us
    dot_general x6, matrix products, dot(): lax.dot_general(left, right, (dims, ((), ())), preferred_element_type=jnp...  11.7 us
    pallas_call x1, Pallas kernels, scatter_rows(): pl.pallas_call(scatter_kernel, out_shape=jax.ShapeDtypeStruct((rows, src....  9.74 us
    dot_general x1, matrix products, per_device(): jnp.dot(both, hit.astype(jnp.bfloat16), preferred_element_type=jnp.float32)  6.5 us
  transfers between devices with their start and end apart: 5, of which 4 were waited for; matrix products, arithmetic and copies ran while one was open for 6% of the time, Pallas kernels for 17%

profile of v2, /device:TPU:0, one launch (start us, length us, event | category | flops | bytes accessed | tf_op | source)
XLA Modules:
  0.0 262.7 jit_solution(1973524553869695565)
XLA Ops:
  7.2 0.0 all-gather.4.cloned.1.call-start
  7.2 0.7 all-gather.4.cloned.1.call-update
  7.9 0.8 reshape.50
  8.7 36.7 %all-gather.4.cloned.1.call-done.src_ref = bf16[8192,128]{1,0:T(8,128)(2,1)} async-done(((bf16[4096,128]{1,0:T(8,128)(2,1)}), bf16[8192,128]{1,0:T(8,128)(2,1)}) %all-gather.4.cloned.1.call-update) | async-done | bytes 2097168 | tf_op jit(solution)/shard_map/all_gather | solution.py:233
  45.4 0.0 copy-start
  45.4 1.6 copy-done
  47.0 6.0 %shard_map.93 = bf16[4096,128]{1,0:T(8,128)(2,1)} custom-call(s32[4096]{0:T(1024)S(1)} %bitcast.46, bf16[8192,128]{1,0:T(8,128)(2,1)S(1)} %copy-done), custom_call_target="tpu_custom_call" | custom-call | bytes 20971520 | tf_op jit(solution)/shard_map/pallas_call | solution.py:31
  53.0 5.6 %all-to-all-start = ((bf16[16,256,128]{2,1,0:T(8,128)(2,1)}), bf16[16,256,128]{2,1,0:T(8,128)(2,1)S(1)}, u32[]{:S(2)}, u32[]{:S(2)}) async-start(bf16[16,256,128]{2,1,0:T(8,128)(2,1)} %bitcast.1), calls=%async_computation | async-start | bytes 2097152 | tf_op jit(solution)/shard_map/all_to_all | solution.py:236
  58.6 0.0 all-gather.6.cloned.1.call-start
  58.7 6.5 %fusion.9 = bf16[768,512]{0,1:T(8,128)(2,1)S(1)} fusion(s32[512]{0:T(512)S(1)} %bitcast.54, bf16[384,4096]{1,0:T(8,128)(2,1)} %param.9, bf16[384,4096]{1,0:T(8,128)(2,1)} %param.8), kind=kOutput, calls=%fused_computation.17 | convolution fusion | flops 3236298752 | bytes 7079936 | tf_op jit(solution)/shard_map/dot_general | solution.py:226
  65.2 0.0 copy-start.1
  65.3 0.6 collective-permute-start
  65.9 10.9 %collective-permute-done = bf16[768,256]{0,1:T(8,128)(2,1)S(1)} collective-permute-done((bf16[768,256]{0,1:T(8,128)(2,1)S(1)}, bf16[768,256]{0,1:T(8,128)(2,1)S(1)}, u32[]{:S(2)}, u32[]{:S(2)}) %collective-permute-start) | collective-permute-done | bytes 393248 | tf_op jit(solution)/shard_map/ppermute | solution.py:84
  76.8 0.0 copy-done.1
  76.8 2.4 convolution_bitcast_fusion.part_ref
  79.2 45.1 %shard_map.94 = bf16[2048,384]{1,0:T(8,128)(2,1)} custom-call(f32[2048,384]{1,0:T(8,128)} %convolution_bitcast_fusion.part_ref), custom_call_target="tpu_custom_call" | custom-call | flops 786432 | bytes 31457280 | tf_op jit(solution)/shard_map/pallas_call | solution.py:209
  124.3 0.0 all-to-all-done
  124.3 2.4 fusion.17.part_ref
  126.7 43.6 %shard_map.95 = bf16[2048,384]{1,0:T(8,128)(2,1)} custom-call(f32[2048,384]{1,0:T(8,128)} %fusion.17.part_ref), custom_call_target="tpu_custom_call" | custom-call | flops 786432 | bytes 31457280 | tf_op jit(solution)/shard_map/pallas_call | solution.py:209
  170.3 0.0 copy-start.2
  170.3 2.1 fusion.25
  172.5 0.4 fusion.12
  172.8 0.0 copy-done.2
  172.8 0.6 fusion.21
  173.5 0.0 copy-start.5
  173.5 0.0 copy-start.4
  173.5 0.1 maximum_multiply_fusion
  173.6 26.7 %all_to_all.18 = f32[16,56,256]{2,1,0:T(8,128)} all-to-all(f32[16,56,256]{2,1,0:T(8,128)S(1)} %maximum_multiply_fusion), channel_id=1, replica_groups=mesh['dp'=16,'tensor'=2] {'dp'}, dimensions={0} | all-to-all | bytes 1835008 | tf_op jit(solution)/shard_map/all_to_all | solution.py:254
  200.3 0.0 all-gather.6.cloned.1.call-update
  200.3 0.0 copy-done.5
  200.3 0.0 copy-start.3
  200.3 1.1 select_reduce_fusion
  201.5 0.9 collective-permute-start.1
  202.4 0.0 copy-done.4
  202.4 2.7 %collective-permute-done.1 = f32[256]{0:T(256)S(1)} collective-permute-done((f32[256]{0:T(256)S(1)}, f32[256]{0:T(256)S(1)}, u32[]{:S(2)}, u32[]{:S(2)}) %collective-permute-start.1) | collective-permute-done | bytes 1056 | tf_op jit(solution)/shard_map/ppermute | solution.py:84
  205.1 2.3 fusion.14
  207.4 0.0 copy-done.3
  207.4 1.8 fusion.8
  209.2 20.6 %all-gather.6.cloned.1.call-done = f32[16,112,256]{2,1,0:T(8,128)} async-done(((f32[16,56,256]{2,1,0:T(8,128)}), f32[16,112,256]{2,1,0:T(8,128)}) %all-gather.6.cloned.1.call-update) | async-done | bytes 1835024 | tf_op jit(solution)/shard_map/all_gather | solution.py:255
  229.8 3.7 %copy.21 = f32[16,2,256,56]{3,2,1,0:T(8,128)} copy(f32[16,2,256,56]{2,3,1,0:T(8,128)} %bitcast.48) | data formatting | bytes 3670016 | tf_op jit(solution)/shard_map/transpose | solution.py:256
  233.5 4.4 %pad.4.src_ref = f32[8192,128]{1,0:T(8,128)} pad(f32[8192,56]{1,0:T(8,128)} %bitcast.47, f32[]{:T(128)} %constant.45.clone.1), padding=0_0x0_72 | pad | bytes 6029316 | tf_op jit(solution)/shard_map/jit(_pad)/pad | solution.py:257
  237.9 9.7 %shard_map.96 = f32[4104,128]{1,0:T(8,128)S(1)} custom-call(s32[8192]{0:T(1024)S(1)} %and_select_fusion.ids_ref, f32[8192,128]{1,0:T(8,128)} %pad.4.src_ref), custom_call_target="tpu_custom_call" | custom-call | bytes 20971520 | tf_op jit(solution)/shard_map/pallas_call | solution.py:62
  247.7 0.1 slice_bitcast_fusion
  247.8 1.8 slice_reduce_fusion
  249.6 2.0 fusion.24
  251.6 2.9 %copy.23 = f32[24,4096]{1,0:T(8,128)} copy(f32[24,4096]{0,1:T(8,128)} %get-tuple-element.16) | data formatting | bytes 786432
  254.5 1.3 copy.22
  (10 shorter events, 0.2 us)
Async XLA Ops:
  7.2 38.2 %all-gather.4.cloned.1.call-start = ((), (), s32[]{:S(2)}) async-start(), calls=%async_computation.2 | async-start | bytes 3145728 | tf_op jit(solution)/shard_map/all_gather | solution.py:233
  45.4 1.6 copy-start
  53.0 71.3 %all-to-all-start = ((bf16[16,256,128]{2,1,0:T(8,128)(2,1)}), bf16[16,256,128]{2,1,0:T(8,128)(2,1)S(1)}, u32[]{:S(2)}, u32[]{:S(2)}) async-start(bf16[16,256,128]{2,1,0:T(8,128)(2,1)} %bitcast.1), calls=%async_computation | async-start | bytes 2097152 | tf_op jit(solution)/shard_map/all_to_all | solution.py:236
  58.6 171.2 %all-gather.6.cloned.1.call-start = ((), (), s32[]{:S(2)}) async-start(), calls=%async_computation.3 | async-start | bytes 2752512 | tf_op jit(solution)/shard_map/all_gather | solution.py:255
  65.2 11.6 %copy-start.1 = (bf16[256,2048]{1,0:T(8,128)(2,1)S(1)}, bf16[256,2048]{1,0:T(8,128)(2,1)}, u32[]{:S(2)}) copy-start(bf16[256,2048]{1,0:T(8,128)(2,1)} %param.6) | copy-start | bytes 3145732
  65.3 11.5 %collective-permute-start = (bf16[768,256]{0,1:T(8,128)(2,1)S(1)}, bf16[768,256]{0,1:T(8,128)(2,1)S(1)}, u32[]{:S(2)}, u32[]{:S(2)}) collective-permute-start(bf16[768,256]{0,1:T(8,128)(2,1)S(1)} %dynamic-slice_bitcast_fusion), channel_id=1, source_target_pairs={{0,1},{1,0},{2,3},{3,2},{4,5},{5,4},{6,7},{7,6},{8,9},{9,8},{10,11... | collective-permute-start | bytes 1179656 | tf_op jit(solution)/shard_map/ppermute | solution.py:84
  170.3 2.5 copy-start.2
  173.5 26.8 %copy-start.5 = (f32[4096]{0:T(1024)S(1)}, f32[4096]{0:T(1024)}, u32[]{:S(2)}) copy-start(f32[4096]{0:T(1024)} %param.10) | copy-start | bytes 49156
  173.5 28.9 %copy-start.4 = (s32[8192]{0:T(1024)S(1)}, s32[8192]{0:T(1024)}, u32[]{:S(2)}) copy-start(s32[8192]{0:T(1024)} %param.7) | copy-start | bytes 98308
  200.3 7.1 %copy-start.3 = (bf16[2048,384]{1,0:T(8,128)(2,1)S(1)}, bf16[2048,384]{1,0:T(8,128)(2,1)}, u32[]{:S(2)}) copy-start(bf16[2048,384]{1,0:T(8,128)(2,1)} %shard_map.94) | copy-start | bytes 4718596
  201.5 3.6 %collective-permute-start.1 = (f32[256]{0:T(256)S(1)}, f32[256]{0:T(256)S(1)}, u32[]{:S(2)}, u32[]{:S(2)}) collective-permute-start(f32[256]{0:T(256)S(1)} %bitcast.56), channel_id=1, source_target_pairs={{0,1},{1,0},{2,3},{3,2},{4,5},{5,4},{6,7},{7,6},{8,9},{9,8},{10,11... | collective-permute-start | bytes 3080 | tf_op jit(solution)/shard_map/ppermute | solution.py:84
Sparse Core Ops, SparseCore 0:
  9.5 35.7 all-gather.3
  200.4 29.3 all-gather.5

commit v3 on v2

--- a/solution.py
+++ b/solution.py
@@ -203,7 +203,7 @@
             collective_id=1, has_side_effects=True, vmem_limit_bytes=56 * 2**20
         ),
         cost_estimate=pl.CostEstimate(
-            flops=samples * rank, bytes_accessed=30 * 2**20, transcendentals=0
+            flops=samples * rank, bytes_accessed=150 * 2**20, transcendentals=0
         ),
     )
     pieces = [call(part[at : at + chunk]) for at in range(0, samples, chunk)]
@@ -231,6 +231,7 @@
     bias_own = to_owner(bias_parts, pair_count, pair_index)
 
     paired = lax.all_gather(upstream, "tensor", axis=0, tiled=True)
+    paired, v_own, u_own = lax.optimization_barrier((paired, v_own, u_own))
     wanted = lax.dynamic_index_in_dim(blocks, pair_index, 1, keepdims=False).reshape(-1)
     wired = gather_rows(wanted, paired, half)
     cotan16 = lax.all_to_all(wired, "dp", split_axis=0, concat_axis=1, tiled=True)
@@ -240,25 +241,39 @@
     scaled = cotan * looked.astype(jnp.float32)
     scaled16 = scaled.astype(jnp.bfloat16)
     sums = jnp.sum(scaled, axis=1)
-    dhrank = all_sum(dot(scaled16, u_own, ((0,), (1,))), dp_count, pair_count)
-
+    dh_part = dot(scaled16, u_own, ((0,), (1,)))
+
+    each = rank // dp_count
+    fill = -(-(each + 3) // 8) * 8 - each
+    terms, rest = [], sums * norm
+    for _ in range(3):
+        term = lax.reduce_precision(rest, exponent_bits=8, mantissa_bits=7)
+        terms.append(term.astype(jnp.bfloat16))
+        rest = rest - term
+    own_b = jnp.pad(jnp.stack(terms), ((0, fill - 3), (0, 0)))
+    own_b = jnp.broadcast_to(own_b[None], (dp_count, fill, own))
+    own_u = (dot(hrank, scaled16, ((0,), (1,))) * norm).astype(jnp.bfloat16)
+    own_u = jnp.concatenate([own_u.reshape(dp_count, each, own), own_b], axis=1)
+    dh_part, own_u = lax.optimization_barrier((dh_part, own_u))
+    came_u = lax.all_to_all(own_u, "dp", split_axis=0, concat_axis=0, tiled=True)
+    dhrank = all_sum(dh_part, dp_count, pair_count)
+    own_v = (dot(dhrank, looked, ((0,), (1,))) * norm).astype(jnp.bfloat16)
+    own_v = own_v.reshape(dp_count, each, own)
     mix = dot(u_own, hrank, ((0,), (1,))) + bias_own[:, None]
     d_looked = (cotan * (mix + 1.0) + dot(v_own, dhrank, ((0,), (1,)))).astype(jnp.bfloat16)
-
-    own_u = dot(hrank, scaled16, ((0,), (1,))).reshape(dp_count, -1, own)
-    own_v = dot(dhrank, looked, ((0,), (1,))).reshape(dp_count, -1, own)
-    each = rank // dp_count
-    fill = -(-(2 * each + 1) // 8) * 8 - 2 * each
-    own_b = jnp.broadcast_to(sums[None, None, :], (dp_count, fill, own))
-    sent = jnp.concatenate([own_u, own_v, own_b], axis=1) * norm
-    came = lax.all_to_all(sent, "dp", split_axis=0, concat_axis=0, tiled=True)
-    full = lax.all_gather(came, "tensor", axis=1, tiled=False)
+    fulls = []
+    came_v = lax.all_to_all(own_v, "dp", split_axis=0, concat_axis=0, tiled=True)
+    for came in (came_u, came_v):
+        fulls.append(lax.all_gather(came, "tensor", axis=1, tiled=False))
+    full = jnp.concatenate(fulls, axis=2).astype(jnp.float32)
     lines = full.transpose(0, 1, 3, 2).reshape(half * pair_count, -1)
     lines = jnp.pad(lines, ((0, 0), (0, 128 - lines.shape[1])))
     place = column_owner - pair_index * half
     place = jnp.where((place >= 0) & (place < half), place, half)
     spread = scatter_rows(place, lines, half + 8)[:half].T
-    return (d_looked, spread[:each], spread[each : 2 * each], spread[2 * each])
+    grad_bias = jnp.sum(spread[each : each + 3], axis=0)
+    grad_v = spread[each + fill : 2 * each + fill]
+    return (d_looked, spread[:each], grad_v, grad_bias)
 
 
 def solution(mesh):

time: 263 us -> 235 us (0.89)
  waiting for transfers between devices: 71.5 us -> 39.4 us
  starting transfers between devices: 7.27 us -> 17.8 us
  blocking collectives: 26.7 us -> 16.3 us
  local copies, waits for them, and re-layouts: 18.8 us -> 11 us
  Pallas kernels: 104 us -> 111 us
  other arithmetic: 1.63 us -> 6.37 us
    all_to_all x1 -> x0, blocking collectives: 26.7 us -> none  [per_device(): came = lax.all_to_all(sent, 'dp', split_axis=0, concat_axis=0, tiled=True)]
    all_gather x1, waiting for transfers between devices: 36.7 us -> 16.1 us  [per_device(): paired = lax.all_gather(upstream, 'tensor', axis=0, tiled=True)]
    all_gather x1 -> x0, waiting for transfers between devices: 20.6 us -> none  [per_device(): full = lax.all_gather(came, 'tensor', axis=1, tiled=False)]
    all_gather x0 -> x2, blocking collectives: none -> 16.3 us  [per_device(): fulls.append(lax.all_gather(came, 'tensor', axis=1, tiled=False))]
    all_to_all x0 -> x2, starting transfers between devices: none -> 7.72 us  [the longest x1 4.19 us: per_device(): lax.all_to_all(own_v, 'dp', split_axis=0, concat_axis=0, tiled=True)]
    pallas_call x2, Pallas kernels: 88.7 us -> 95.3 us  [all_sum(): pieces = [call(part[at:at + chunk]) for at in range(0, samples, chunk)]]
    ppermute x2, waiting for transfers between devices: 13.6 us -> 18.4 us  [to_owner(): lax.ppermute(sent, 'tensor', [(i, (i + shift) % pair_count) for i in rang...]
    pad x1 -> x0, local copies, waits for them, and re-layouts: 4.44 us -> none  [per_device(): lines = jnp.pad(lines, ((0, 0), (0, 128 - lines.shape[1])))]
  transfers between devices with their start and end apart: 5 -> 6, of which waited for: 4 -> 4; matrix products, arithmetic and copies ran while one was open for 6% -> 6% of each run, Pallas kernels for 17% -> 22%
where the time goes in v3:
time: 235 us
  Pallas kernels  111 us (47%)
  waiting for transfers between devices  39.4 us (17%)
  matrix products  18.5 us (8%)
  starting transfers between devices  17.8 us (8%)
  blocking collectives  16.3 us (7%)
  between operations  14.3 us (6%)
  local copies, waits for them, and re-layouts  11 us (5%)
  other arithmetic  6.37 us (3%)
    pallas_call x2, Pallas kernels, all_sum(): pieces = [call(part[at:at + chunk]) for at in range(0, samples, chunk)]  95.3 us
    ppermute x2, waiting for transfers between devices, to_owner(): lax.ppermute(sent, 'tensor', [(i, (i + shift) % pair_count) for i in rang...  18.4 us
    all_gather x2, blocking collectives, per_device(): fulls.append(lax.all_gather(came, 'tensor', axis=1, tiled=False))  16.3 us
    all_gather x1, waiting for transfers between devices, per_device(): paired = lax.all_gather(upstream, 'tensor', axis=0, tiled=True)  16.1 us
    dot_general x6, matrix products, dot(): lax.dot_general(left, right, (dims, ((), ())), preferred_element_type=jnp...  12 us
    pallas_call x1, Pallas kernels, scatter_rows(): pl.pallas_call(scatter_kernel, out_shape=jax.ShapeDtypeStruct((rows, src....  9.74 us
    unnamed x15, local copies, waits for them, and re-layouts  6.86 us
    dot_general x1, matrix products, per_device(): jnp.dot(both, hit.astype(jnp.bfloat16), preferred_element_type=jnp.float32)  6.5 us
  transfers between devices with their start and end apart: 6, of which 4 were waited for; matrix products, arithmetic and copies ran while one was open for 6% of the time, Pallas kernels for 22%

profile of v3, /device:TPU:0, one launch (start us, length us, event | category | flops | bytes accessed | tf_op | source)
XLA Modules:
  0.0 234.6 jit_solution(14208873239117397206)
XLA Ops:
  7.2 0.0 all-gather.4.cloned.1.call-start
  7.2 0.7 all-gather.4.cloned.1.call-update
  7.9 0.8 reshape.92
  8.7 6.5 %fusion.7 = bf16[768,512]{0,1:T(8,128)(2,1)S(1)} fusion(s32[512]{0:T(512)S(1)} %bitcast.65, bf16[384,4096]{1,0:T(8,128)(2,1)} %param.9, bf16[384,4096]{1,0:T(8,128)(2,1)} %param.8), kind=kOutput, calls=%fused_computation.16 | convolution fusion | flops 3236298752 | bytes 7079936 | tf_op jit(solution)/shard_map/dot_general | solution.py:226
  15.3 3.0 %collective-permute-start = (bf16[768,256]{0,1:T(8,128)(2,1)S(1)}, bf16[768,256]{0,1:T(8,128)(2,1)S(1)}, u32[]{:S(2)}, u32[]{:S(2)}) collective-permute-start(bf16[768,256]{0,1:T(8,128)(2,1)S(1)} %dynamic-slice_bitcast_fusion), channel_id=1, source_target_pairs={{0,1},{1,0},{2,3},{3,2},{4,5},{5,4},{6,7},{7,6},{8,9},{9,8},{10,11... | collective-permute-start | bytes 1179656 | tf_op jit(solution)/shard_map/ppermute | solution.py:84
  18.3 15.6 %collective-permute-done = bf16[768,256]{0,1:T(8,128)(2,1)S(1)} collective-permute-done((bf16[768,256]{0,1:T(8,128)(2,1)S(1)}, bf16[768,256]{0,1:T(8,128)(2,1)S(1)}, u32[]{:S(2)}, u32[]{:S(2)}) %collective-permute-start) | collective-permute-done | bytes 393248 | tf_op jit(solution)/shard_map/ppermute | solution.py:84
  34.0 16.1 %all-gather.4.cloned.1.call-done.src_ref = bf16[8192,128]{1,0:T(8,128)(2,1)} async-done(((bf16[4096,128]{1,0:T(8,128)(2,1)}), bf16[8192,128]{1,0:T(8,128)(2,1)}) %all-gather.4.cloned.1.call-update) | async-done | bytes 2097168 | tf_op jit(solution)/shard_map/all_gather | solution.py:233
  50.1 0.0 copy-start
  50.1 1.6 copy-done
  51.7 0.0 copy-start.1
  51.7 6.0 %shard_map.93 = bf16[4096,128]{1,0:T(8,128)(2,1)} custom-call(s32[4096]{0:T(1024)S(1)} %bitcast.56, bf16[8192,128]{1,0:T(8,128)(2,1)S(1)} %copy-done), custom_call_target="tpu_custom_call" | custom-call | bytes 20971520 | tf_op jit(solution)/shard_map/pallas_call | solution.py:31
  57.7 6.2 %all-to-all-start = ((bf16[16,256,128]{2,1,0:T(8,128)(2,1)}), bf16[16,256,128]{2,1,0:T(8,128)(2,1)S(1)}, u32[]{:S(2)}, u32[]{:S(2)}) async-start(bf16[16,256,128]{2,1,0:T(8,128)(2,1)} %bitcast.4), calls=%async_computation | async-start | bytes 2097152 | tf_op jit(solution)/shard_map/all_to_all | solution.py:237
  63.9 0.0 copy-done.1
  63.9 2.4 %convolution_bitcast_fusion.part_ref = f32[2048,384]{1,0:T(8,128)} fusion(bf16[384,256]{0,1:T(8,128)(2,1)S(1)} %get-tuple-element.11, bf16[256,2048]{1,0:T(8,128)(2,1)S(1)} %copy-done.1), kind=kOutput, calls=%fused_computation.7 | convolution fusion | flops 402653184 | bytes 4390912 | tf_op jit(solution)/shard_map/dot_general | solution.py:76
  66.3 51.4 %shard_map.94 = bf16[2048,384]{1,0:T(8,128)(2,1)} custom-call(f32[2048,384]{1,0:T(8,128)} %convolution_bitcast_fusion.part_ref), custom_call_target="tpu_custom_call" | custom-call | flops 786432 | bytes 157286400 | tf_op jit(solution)/shard_map/pallas_call | solution.py:209
  117.6 0.0 all-to-all-done
  117.6 0.0 copy-start.2
  117.7 0.4 fusion.10
  118.1 1.0 copy-done.2
  119.1 0.6 fusion.12
  119.7 0.7 pad_maximum_fusion
  120.5 2.4 %fusion.23.part_ref = f32[2048,384]{1,0:T(8,128)} fusion(bf16[384,256]{0,1:T(8,128)(2,1)S(1)} %get-tuple-element.10, bf16[256,2048]{1,0:T(8,128)(2,1)S(1)} %copy-done.1, bf16[16,256,128]{2,1,0:T(8,128)(2,1)S(1)} %all-to-all-done), kind=kOutput, calls=%fused_computation.46 | convolution fusion | flops 404750336 | bytes 5439488 | tf_op jit(solution)/shard_map/dot_general | solution.py:76
  122.8 44.0 %shard_map.95 = bf16[2048,384]{1,0:T(8,128)(2,1)} custom-call(f32[2048,384]{1,0:T(8,128)} %fusion.23.part_ref), custom_call_target="tpu_custom_call" | custom-call | flops 786432 | bytes 157286400 | tf_op jit(solution)/shard_map/pallas_call | solution.py:209
  166.8 0.0 copy-start.5
  166.9 0.0 copy-start.4
  166.9 2.7 %fusion.13 = bf16[384,256]{1,0:T(8,128)(2,1)} fusion(bf16[2048,384]{1,0:T(8,128)(2,1)} %shard_map.95, bf16[256,2048]{1,0:T(8,128)(2,1)S(1)} %copy-done.1), kind=kOutput, calls=%fused_computation.22 | convolution fusion | flops 402849792 | bytes 2818048 | tf_op jit(solution)/shard_map/dot_general | solution.py:76
  169.6 4.2 %all-to-all-start.2 = ((bf16[16,24,256]{2,1,0:T(8,128)(2,1)}), bf16[16,24,256]{2,1,0:T(8,128)(2,1)S(1)}, u32[]{:S(2)}, u32[]{:S(2)}) async-start(bf16[16,24,256]{2,1,0:T(8,128)(2,1)} %bitcast.12), calls=%async_computation.2 | async-start | bytes 393216 | tf_op jit(solution)/shard_map/all_to_all | solution.py:265
  173.8 0.0 copy-done.5
  173.8 1.1 select_reduce_fusion
  175.0 0.9 collective-permute-start.1
  175.8 0.0 copy-done.4
  175.8 2.8 %collective-permute-done.1 = f32[256]{0:T(256)S(1)} collective-permute-done((f32[256]{0:T(256)S(1)}, f32[256]{0:T(256)S(1)}, u32[]{:S(2)}, u32[]{:S(2)}) %collective-permute-start.1) | collective-permute-done | bytes 1056 | tf_op jit(solution)/shard_map/ppermute | solution.py:84
  178.6 0.0 copy-start.3
  178.6 4.2 %all-to-all-done.2 = bf16[16,24,256]{2,1,0:T(8,128)(2,1)S(1)} async-done(((bf16[16,24,256]{2,1,0:T(8,128)(2,1)}), bf16[16,24,256]{2,1,0:T(8,128)(2,1)S(1)}, u32[]{:S(2)}, u32[]{:S(2)}) %all-to-all-start.2) | async-done | bytes 196640 | tf_op jit(solution)/shard_map/all_to_all | solution.py:265
  182.8 3.5 %all-to-all-start.1 = ((bf16[16,32,256]{2,1,0:T(8,128)(2,1)}), bf16[16,32,256]{2,1,0:T(8,128)(2,1)S(1)}, u32[]{:S(2)}, u32[]{:S(2)}) async-start(bf16[16,32,256]{2,1,0:T(8,128)(2,1)} %pad_maximum_fusion), calls=%async_computation.1 | async-start | bytes 524288 | tf_op jit(solution)/shard_map/all_to_all | solution.py:258
  186.3 2.1 fusion.27
  188.5 0.0 copy-done.3
  188.5 1.8 fusion.6
  190.2 7.8 %all-gather.1 = bf16[16,48,256]{2,1,0:T(8,128)(2,1)S(1)} all-gather(bf16[16,24,256]{2,1,0:T(8,128)(2,1)S(1)} %all-to-all-done.2), channel_id=3, replica_groups=mesh['dp'=16,'tensor'=2] {'tensor'}, dimensions={1}, use_global_device_ids=true | all-gather | bytes 589824 | tf_op jit(solution)/shard_map/all_gather | solution.py:267
  198.0 0.0 all-to-all-done.1
  198.0 8.5 %all-gather = bf16[16,64,256]{2,1,0:T(8,128)(2,1)S(1)} all-gather(bf16[16,32,256]{2,1,0:T(8,128)(2,1)S(1)} %all-to-all-done.1), channel_id=2, replica_groups=mesh['dp'=16,'tensor'=2] {'tensor'}, dimensions={1}, use_global_device_ids=true | all-gather | bytes 786432 | tf_op jit(solution)/shard_map/all_gather | solution.py:267
  206.5 0.1 maximum_bitcast_fusion
  206.6 1.1 copy.21
  207.7 2.2 pad_convert_fusion.src_ref
  209.9 9.7 %shard_map.96 = f32[4104,128]{1,0:T(8,128)S(1)} custom-call(s32[8192]{0:T(1024)S(1)} %and_select_fusion.ids_ref, f32[8192,128]{1,0:T(8,128)} %pad_convert_fusion.src_ref), custom_call_target="tpu_custom_call" | custom-call | bytes 20971520 | tf_op jit(solution)/shard_map/pallas_call | solution.py:62
  219.6 0.1 slice_bitcast_fusion
  219.8 2.0 fusion.25
  221.8 1.8 slice_reduce_fusion
  223.6 2.9 %copy.22 = f32[24,4096]{1,0:T(8,128)} copy(f32[24,4096]{0,1:T(8,128)} %get-tuple-element.27) | data formatting | bytes 786432
  226.5 1.3 copy.23
  (14 shorter events, 0.2 us)
Async XLA Ops:
  7.2 43.0 %all-gather.4.cloned.1.call-start = ((), (), s32[]{:S(2)}) async-start(), calls=%async_computation.3 | async-start | bytes 3145728 | tf_op jit(solution)/shard_map/all_gather | solution.py:233
  15.3 18.6 %collective-permute-start = (bf16[768,256]{0,1:T(8,128)(2,1)S(1)}, bf16[768,256]{0,1:T(8,128)(2,1)S(1)}, u32[]{:S(2)}, u32[]{:S(2)}) collective-permute-start(bf16[768,256]{0,1:T(8,128)(2,1)S(1)} %dynamic-slice_bitcast_fusion), channel_id=1, source_target_pairs={{0,1},{1,0},{2,3},{3,2},{4,5},{5,4},{6,7},{7,6},{8,9},{9,8},{10,11... | collective-permute-start | bytes 1179656 | tf_op jit(solution)/shard_map/ppermute | solution.py:84
  50.1 1.6 copy-start
  51.7 12.2 %copy-start.1 = (bf16[256,2048]{1,0:T(8,128)(2,1)S(1)}, bf16[256,2048]{1,0:T(8,128)(2,1)}, u32[]{:S(2)}) copy-start(bf16[256,2048]{1,0:T(8,128)(2,1)} %param.6) | copy-start | bytes 3145732
  57.7 59.9 %all-to-all-start = ((bf16[16,256,128]{2,1,0:T(8,128)(2,1)}), bf16[16,256,128]{2,1,0:T(8,128)(2,1)S(1)}, u32[]{:S(2)}, u32[]{:S(2)}) async-start(bf16[16,256,128]{2,1,0:T(8,128)(2,1)} %bitcast.4), calls=%async_computation | async-start | bytes 2097152 | tf_op jit(solution)/shard_map/all_to_all | solution.py:237
  117.6 1.4 copy-start.2
  166.8 6.9 %copy-start.5 = (f32[4096]{0:T(1024)S(1)}, f32[4096]{0:T(1024)}, u32[]{:S(2)}) copy-start(f32[4096]{0:T(1024)} %param.10) | copy-start | bytes 49156
  166.9 9.0 %copy-start.4 = (s32[8192]{0:T(1024)S(1)}, s32[8192]{0:T(1024)}, u32[]{:S(2)}) copy-start(s32[8192]{0:T(1024)} %param.7) | copy-start | bytes 98308
  169.6 13.2 %all-to-all-start.2 = ((bf16[16,24,256]{2,1,0:T(8,128)(2,1)}), bf16[16,24,256]{2,1,0:T(8,128)(2,1)S(1)}, u32[]{:S(2)}, u32[]{:S(2)}) async-start(bf16[16,24,256]{2,1,0:T(8,128)(2,1)} %bitcast.12), calls=%async_computation.2 | async-start | bytes 393216 | tf_op jit(solution)/shard_map/all_to_all | solution.py:265
  175.0 3.6 %collective-permute-start.1 = (f32[256]{0:T(256)S(1)}, f32[256]{0:T(256)S(1)}, u32[]{:S(2)}, u32[]{:S(2)}) collective-permute-start(f32[256]{0:T(256)S(1)} %bitcast.67), channel_id=1, source_target_pairs={{0,1},{1,0},{2,3},{3,2},{4,5},{5,4},{6,7},{7,6},{8,9},{9,8},{10,11... | collective-permute-start | bytes 3080 | tf_op jit(solution)/shard_map/ppermute | solution.py:84
  178.6 9.9 %copy-start.3 = (bf16[2048,384]{1,0:T(8,128)(2,1)S(1)}, bf16[2048,384]{1,0:T(8,128)(2,1)}, u32[]{:S(2)}) copy-start(bf16[2048,384]{1,0:T(8,128)(2,1)} %shard_map.95) | copy-start | bytes 4718596
  182.8 15.2 %all-to-all-start.1 = ((bf16[16,32,256]{2,1,0:T(8,128)(2,1)}), bf16[16,32,256]{2,1,0:T(8,128)(2,1)S(1)}, u32[]{:S(2)}, u32[]{:S(2)}) async-start(bf16[16,32,256]{2,1,0:T(8,128)(2,1)} %pad_maximum_fusion), calls=%async_computation.1 | async-start | bytes 524288 | tf_op jit(solution)/shard_map/all_to_all | solution.py:258
Sparse Core Ops, SparseCore 0:
  9.5 40.5 all-gather.3
